TPU v7x, 128 devices: a whole 4x4x4 slice. The times are simulated.
128 devices in a mesh: lat: 8 (over z, core), lon: 16 (over x, y).
Axes of the slice: x: 4, y: 4, z: 4, core: 2. Of those that a mesh axis runs over, the one named last changes fastest.
Arguments:
- grid_latent: bfloat16 [64, 2048, 512], P('lat', 'lon'), may hold values from -6 to 6
- mesh_latent: bfloat16 [8, 16, 320, 512], P('lat', 'lon'), may hold values from -6 to 6
- edge_latent: bfloat16 [8, 16, 2560, 512], P('lat', 'lon'), may hold values from -6 to 6
- g2m_src: int32 [8, 16, 1536], P('lat', 'lon'), may hold values from 0 to 1583, as said below
- g2m_dst: int32 [8, 16, 1536], P('lat', 'lon'), may hold values from 0 to 319
- g2m_count: int32 [8, 16], P('lat', 'lon'), may hold values from 577 to 1536, as said below
- mesh_src: int32 [8, 16, 2560], P('lat', 'lon'), may hold values from 0 to 4927, as said below
- mesh_dst: int32 [8, 16, 2560], P('lat', 'lon'), may hold values from 0 to 319
- m2g_src: int32 [3, 64, 2048], P(None, 'lat', 'lon'), may hold values from 0 to 2879, as said below
- weights_in: bfloat16 [18, 512, 512], replicated, may hold values from -0.25 to 0.25
- weights_out: bfloat16 [8, 512, 512], replicated, may hold values from -0.25 to 0.25
- gains: float32 [8, 512], replicated, may hold values from 0.25 to 1.75
Outputs:
- grid_out: bfloat16 [64, 2048, 512], P('lat', 'lon')
Inputs may be any that keep to these rules, and one draw needn't show every extreme that they name: `g2m_src`: live slots read only cells of the widened tile that lie inside the latitude range of the grid (no cell beyond a pole). `g2m_count`: the first and last latitude bands fill all 1536 slots. `mesh_src`: A sender below 2880 is node j of nine-patch block k (index k * 320 + j); for k other than 4 the block lies inside the latitude range and j < 64. A sender of 2880 or more is a coarse node: the last 16 nodes of every patch in patch order. `m2g_src`: index k * 320 + j into the nine patches around the cell's tile; for k other than 4 the patch lies inside the latitude range and j < 64.
All inputs are finite; a program needn't handle non-finite values.
Results may differ from a plain program's by a relative error of at most 0.017.
Values may be sent and summed in bfloat16 or wider, within the bound.
A program may use at most 128 MiB of HBM per device.

v0:
```python
import jax
import jax.numpy as jnp
from jax import lax
from jax.sharding import PartitionSpec as P

L = 512
HALO = 2
MESH = 320
COARSE = 16
ROUNDS = 2


epsilon = 1e-05


def extended(block, sides, width):
    for axis, dim in sides:
        count = lax.axis_size(axis)
        forward = [(i, i + 1) for i in range(count - 1)]
        forward.append((count - 1, 0))
        backward = [(target, source) for source, target in forward]
        low = lax.ppermute(
            lax.slice_in_dim(block, block.shape[dim] - width, None, axis=dim), axis, forward
        )
        high = lax.ppermute(lax.slice_in_dim(block, 0, width, axis=dim), axis, backward)
        block = jnp.concatenate([low, block, high], axis=dim)
    return block


def finish(before, w_out, gain):
    hidden = jax.nn.silu(before).astype(jnp.bfloat16)
    result = jnp.dot(hidden, w_out, preferred_element_type=jnp.float32)
    centre = jnp.mean(result, axis=-1, keepdims=True)
    centred = result - centre
    spread = jnp.mean(centred * centred, axis=-1, keepdims=True)
    return centred * lax.rsqrt(spread + epsilon) * gain


def project(rows_in, weight):
    return jnp.dot(rows_in, weight, preferred_element_type=jnp.float32)


def update_node(node_rows, totals, w_self, w_total, w_out, gain):
    before = project(node_rows, w_self) + project(totals, w_total)
    return (node_rows.astype(jnp.float32) + finish(before, w_out, gain)).astype(jnp.bfloat16)


def near_rows(mesh_shard):
    rim_rows = extended(mesh_shard, (("lat", 0), ("lon", 1)), 1)
    return rim_rows.reshape(-1, L)


def coarse_rows(mesh_shard):
    own_coarse = mesh_shard[0, 0, MESH - COARSE :]
    return lax.all_gather(own_coarse, ("lat", "lon"), axis=0, tiled=True)


def encode(grid_tile, mesh_own, senders, targets, live_count, weights_in, weights_out, gains):
    grid_proj = project(grid_tile, weights_in[0])
    mesh_proj = project(mesh_own, weights_in[1])
    node_ids = jnp.arange(MESH, dtype=jnp.int32)
    message = finish(grid_proj[senders] + mesh_proj[targets], weights_out[0], gains[0]).astype(
        jnp.bfloat16
    )
    alive = jnp.arange(senders.shape[0], dtype=jnp.int32) < live_count
    onehot = ((targets[None, :] == node_ids[:, None]) & alive[None, :]).astype(jnp.bfloat16)
    totals = jnp.dot(onehot, message, preferred_element_type=jnp.float32)
    return update_node(
        mesh_own,
        totals.astype(jnp.bfloat16),
        weights_in[2],
        weights_in[3],
        weights_out[1],
        gains[1],
    )


def process(
    table, mesh_own, edge_rows, senders, targets, weights_in, weights_out, gains, layer_index
):
    first_slot = 4 + 5 * layer_index
    sender_proj = project(table, weights_in[first_slot + 1])
    before = (
        project(edge_rows, weights_in[first_slot])
        + sender_proj[senders]
        + project(mesh_own, weights_in[first_slot + 2])[targets]
    )
    edges_new = (
        edge_rows.astype(jnp.float32)
        + finish(before, weights_out[2 + 2 * layer_index], gains[2 + 2 * layer_index])
    ).astype(jnp.bfloat16)
    node_ids = jnp.arange(MESH, dtype=jnp.int32)
    onehot = (targets[None, :] == node_ids[:, None]).astype(jnp.bfloat16)
    totals = jnp.dot(onehot, edges_new, preferred_element_type=jnp.float32)
    mesh_new = update_node(
        mesh_own,
        totals.astype(jnp.bfloat16),
        weights_in[first_slot + 3],
        weights_in[first_slot + 4],
        weights_out[3 + 2 * layer_index],
        gains[3 + 2 * layer_index],
    )
    return (mesh_new, edges_new)


def decode(table, grid_own, corners, weights_in, weights_out, gains):
    last_in = 4 + 5 * ROUNDS
    last_out = 2 + 2 * ROUNDS
    sender_proj = project(table, weights_in[last_in])
    own_proj = project(grid_own, weights_in[last_in + 1])
    totals = jnp.zeros(own_proj.shape, jnp.float32)
    for corner in range(3):
        totals = totals + finish(
            sender_proj[corners[corner]] + own_proj, weights_out[last_out], gains[last_out]
        )
    return update_node(
        grid_own,
        totals.astype(jnp.bfloat16),
        weights_in[last_in + 2],
        weights_in[last_in + 3],
        weights_out[last_out + 1],
        gains[last_out + 1],
    )


def on_device(
    grid_latent,
    mesh_latent,
    edge_latent,
    g2m_src,
    g2m_dst,
    g2m_count,
    mesh_src,
    mesh_dst,
    m2g_src,
    weights_in,
    weights_out,
    gains,
):
    grid_tile = extended(grid_latent, (("lat", 0), ("lon", 1)), HALO).reshape(-1, L)
    mesh_own = encode(
        grid_tile,
        mesh_latent[0, 0],
        g2m_src[0, 0],
        g2m_dst[0, 0],
        g2m_count[0, 0],
        weights_in,
        weights_out,
        gains,
    )
    edge_rows = edge_latent[0, 0]
    mesh_senders = mesh_src[0, 0]
    targets = mesh_dst[0, 0]
    for layer_index in range(ROUNDS):
        mesh_shard = mesh_own[None, None]
        table = jnp.concatenate([near_rows(mesh_shard), coarse_rows(mesh_shard)], axis=0)
        mesh_own, edge_rows = process(
            table,
            mesh_own,
            edge_rows,
            mesh_senders,
            targets,
            weights_in,
            weights_out,
            gains,
            layer_index,
        )
    table = near_rows(mesh_own[None, None])
    grid_own = grid_latent.reshape(-1, L)
    corners = m2g_src.reshape(3, -1)
    result = decode(table, grid_own, corners, weights_in, weights_out, gains)
    return result.reshape(grid_latent.shape)


def solution(mesh):
    placed = (
        P("lat", "lon", None),
        P("lat", "lon", None, None),
        P("lat", "lon", None, None),
        P("lat", "lon", None),
        P("lat", "lon", None),
        P("lat", "lon"),
        P("lat", "lon", None),
        P("lat", "lon", None),
        P(None, "lat", "lon"),
        P(),
        P(),
        P(),
    )
    return jax.shard_map(
        on_device, mesh=mesh, in_specs=placed, out_specs=P("lat", "lon", None), check_vma=False
    )
```

profile of v0, /device:TPU:0, one launch (start us, length us, event | category | flops | bytes accessed | tf_op | source)
XLA Modules:
  0.0 356.1 jit_solution(11525937119771249328)
XLA Ops:
  6.6 1.1 fusion.153
  7.8 3.6 %collective-permute-start.1 = (bf16[2,128,512]{2,1,0:T(8,128)(2,1)S(1)}, bf16[2,128,512]{2,1,0:T(8,128)(2,1)S(1)}, u32[]{:S(2)}, u32[]{:S(2)}) collective-permute-start(bf16[2,128,512]{2,1,0:T(8,128)(2,1)S(1)} %get-tuple-element.7), channel_id=1, source_target_pairs={{16,0},{32,16},{48,32},{64,48},{80,64},{96,80},{112,96},{0,112},{1... | collective-permute-start | bytes 786440 | tf_op jit(solution)/shard_map/ppermute | solution.py:25
  11.3 1.5 fusion.97
  12.8 2.3 fusion.101
  16.7 1.6 collective-permute-start.2
  18.3 3.8 %collective-permute-start.3 = (bf16[12,2,512]{2,1,0:T(2,128)(2,1)S(1)}, bf16[12,2,512]{2,1,0:T(2,128)(2,1)S(1)}, u32[]{:S(2)}, u32[]{:S(2)}) collective-permute-start(bf16[12,2,512]{2,1,0:T(2,128)(2,1)S(1)} %get-tuple-element.6), channel_id=1, source_target_pairs={{1,0},{2,1},{3,2},{4,3},{5,4},{6,5},{7,6},{8,7},{9,8},{10,9},{11,1... | collective-permute-start | bytes 73736 | tf_op jit(solution)/shard_map/ppermute | solution.py:25
  22.1 5.0 %gather_fusion.1 = f32[1536,512]{1,0:T(8,128)} fusion(f32[320,512]{1,0:T(8,128)S(1)} %fusion.97, s32[2048]{0:T(1024)S(1)} %get-tuple-element.40), kind=kCustom, calls=%fused_computation.1 | custom fusion | bytes 6297600 | tf_op jit(solution)/shard_map/gather | solution.py:62
  27.7 1.8 reshape.348
  29.5 2.5 fusion.99
  32.1 5.0 %gather_fusion = f32[1536,512]{1,0:T(8,128)} fusion(f32[1584,512]{1,0:T(8,128)S(1)} %fusion.99, s32[2048]{0:T(1024)S(1)} %get-tuple-element.41), kind=kCustom, calls=%fused_computation | custom fusion | bytes 6297600 | tf_op jit(solution)/shard_map/gather | solution.py:62
  37.0 4.1 %fusion.156 = (f32[1536]{0:T(1024)S(1)}, f32[1536,512]{0,1:T(8,128)S(1)}) fusion(bf16[8,512,512]{2,1,0:T(8,128)(2,1)} %param.22, f32[1536,512]{1,0:T(8,128)} %gather_fusion, f32[1536,512]{1,0:T(8,128)} %gather_fusion.1), kind=kOutput, calls=%fused_computation.216 | convolution fusion | flops 810809856 | bytes 9967616 | tf_op jit(solution)/shard_map/dot_general | solution.py:32
  41.5 3.3 multiply_convert_fusion.24
  44.8 1.6 fusion.157
  47.6 2.9 collective-permute-start.5
  50.5 4.8 %collective-permute-done.4 = bf16[1,1,320,512]{3,2,1,0:T(8,128)(2,1)S(1)} collective-permute-done((bf16[1,1,320,512]{3,2,1,0:T(8,128)(2,1)S(1)}, bf16[1,1,320,512]{3,2,1,0:T(8,128)(2,1)S(1)}, u32[]{:S(2)}, u32[]{:S(2)}) %collective-permute-start.4) | collective-permute-done | bytes 327712 | tf_op jit(solution)/shard_map/ppermute | solution.py:22
  55.3 1.1 pad_maximum_fusion.4
  56.3 5.5 %collective-permute-start.7 = (bf16[3,1,320,512]{3,2,1,0:T(8,128)(2,1)}, bf16[3,1,320,512]{3,2,1,0:T(8,128)(2,1)}, u32[]{:S(2)}, u32[]{:S(2)}) collective-permute-start(bf16[3,1,320,512]{3,2,1,0:T(8,128)(2,1)} %pad_maximum_fusion.4), channel_id=1, source_target_pairs={{1,0},{2,1},{3,2},{4,3},{5,4},{6,5},{7,6},{8,7},{9,8},{10,9},{11,1... | collective-permute-start | bytes 2949128 | tf_op jit(solution)/shard_map/ppermute | solution.py:25
  61.8 4.4 %copy.14 = bf16[1,1,2560,512]{2,3,1,0:T(8,128)(2,1)} copy(bf16[1,1,2560,512]{3,2,1,0:T(8,128)(2,1)} %param.14) | data formatting | bytes 5242880 | tf_op args[2]
  66.4 1.4 fusion.86
  67.7 7.5 %gather_fusion.3 = f32[2560,512]{1,0:T(8,128)} fusion(f32[320,512]{1,0:T(8,128)S(1)} %fusion.86, s32[3072]{0:T(1024)S(1)} %pad_clamp_fusion), kind=kCustom, calls=%fused_computation.3 | custom fusion | bytes 10496000 | tf_op jit(solution)/shard_map/gather | solution.py:86
  75.2 1.4 fusion.91
  76.6 6.7 %collective-permute-done.6 = bf16[3,1,320,512]{3,2,1,0:T(8,128)(2,1)S(1)} collective-permute-done((bf16[3,1,320,512]{3,2,1,0:T(8,128)(2,1)}, bf16[3,1,320,512]{3,2,1,0:T(8,128)(2,1)S(1)}, u32[]{:S(2)}, u32[]{:S(2)}) %collective-permute-start.6) | collective-permute-done | bytes 983072 | tf_op jit(solution)/shard_map/ppermute | solution.py:22
  83.3 2.8 pad_maximum_fusion
  86.1 27.3 %all-gather.5.cloned.1.call-done = bf16[1,1,2048,512]{3,2,1,0:T(8,128)(2,1)} async-done(((bf16[1,1,16,512]{3,2,1,0:T(8,128)(2,1)}), bf16[1,1,2048,512]{3,2,1,0:T(8,128)(2,1)}) %all-gather.5.cloned.1.call-update) | async-done | bytes 2097168 | tf_op jit(solution)/shard_map/all_gather | solution.py:55
  113.4 9.2 %fusion = f32[4928,512]{1,0:T(8,128)} fusion(bf16[2048,512]{1,0:T(8,128)(2,1)} %bitcast.206, bf16[2880,512]{1,0:T(8,128)(2,1)} %bitcast.190, bf16[18,512,512]{2,1,0:T(8,128)(2,1)} %param.21), kind=kOutput, calls=%fused_computation.15 | convolution fusion | flops 2593783808 | bytes 15663104 | tf_op jit(solution)/shard_map/dot_general | solution.py:40
  122.5 12.5 %gather_fusion.2 = f32[2560,512]{1,0:T(8,128)} fusion(f32[4928,512]{1,0:T(8,128)} %fusion, s32[3072]{0:T(1024)S(1)} %pad_clamp_fusion.1), kind=kCustom, calls=%fused_computation.2 | custom fusion | bytes 10496000 | tf_op jit(solution)/shard_map/gather | solution.py:85
  135.1 10.9 %fusion.158 = (f32[2560]{0:T(1024)S(1)}, f32[2560,512]{0,1:T(8,128)}) fusion(bf16[8,512,512]{2,1,0:T(8,128)(2,1)} %param.22, f32[2560,512]{1,0:T(8,128)} %gather_fusion.3, f32[2560,512]{1,0:T(8,128)} %gather_fusion.2, bf16[1,1,2560,512]{3,2,1,0:T(8,128)(2,1)} %param.14, bf16[18,512,512]{2,1,0:T(8,128)(2,1)} %param.21), kind=kOutput, calls=%fused_computation.218 | convolution fusion | flops 2694837760 | bytes 19408896 | tf_op jit(solution)/shard_map/dot_general | solution.py:32
  146.0 3.2 multiply_reduce_fusion.1
  150.0 4.5 %add_convert_fusion.1 = bf16[2560,512]{0,1:T(8,128)(2,1)} fusion(f32[2560,512]{0,1:T(8,128)S(1)} %copy-done.2, bf16[1,1,2560,512]{2,3,1,0:T(8,128)(2,1)} %copy.14, f32[512]{0:T(512)S(1)} %bitcast.201, f32[2560]{0:T(1024)S(1)} %add_rsqrt_fusion.1, f32[2560]{0:T(1024)S(1)} %broadcast_multiply_fusion.1), kind=kLoop, calls=%fused_computation.12 | loop fusion | flops 7864320 | bytes 10508288 | tf_op jit(solution)/shard_map/convert_element_type | solution.py:91
  154.6 3.2 multiply_convert_fusion.23
  157.8 1.5 fusion.163
  160.6 2.7 collective-permute-start.9
  163.3 4.8 %collective-permute-done.8 = bf16[1,1,320,512]{3,2,1,0:T(8,128)(2,1)S(1)} collective-permute-done((bf16[1,1,320,512]{3,2,1,0:T(8,128)(2,1)S(1)}, bf16[1,1,320,512]{3,2,1,0:T(8,128)(2,1)S(1)}, u32[]{:S(2)}, u32[]{:S(2)}) %collective-permute-start.8) | collective-permute-done | bytes 327712 | tf_op jit(solution)/shard_map/ppermute | solution.py:22
  168.1 1.1 pad_maximum_fusion.5
  169.6 5.1 %collective-permute-start.11 = (bf16[3,1,320,512]{3,2,1,0:T(8,128)(2,1)}, bf16[3,1,320,512]{3,2,1,0:T(8,128)(2,1)}, u32[]{:S(2)}, u32[]{:S(2)}) collective-permute-start(bf16[3,1,320,512]{3,2,1,0:T(8,128)(2,1)} %pad_maximum_fusion.5), channel_id=1, source_target_pairs={{1,0},{2,1},{3,2},{4,3},{5,4},{6,5},{7,6},{8,7},{9,8},{10,9},{11,1... | collective-permute-start | bytes 2949128 | tf_op jit(solution)/shard_map/ppermute | solution.py:25
  174.7 1.4 fusion.75
  176.1 7.5 %gather_fusion.5 = f32[2560,512]{1,0:T(8,128)} fusion(f32[320,512]{1,0:T(8,128)S(1)} %fusion.75, s32[3072]{0:T(1024)S(1)} %pad_clamp_fusion), kind=kCustom, calls=%fused_computation.5 | custom fusion | bytes 10496000 | tf_op jit(solution)/shard_map/gather | solution.py:86
  183.6 1.4 fusion.80
  184.9 11.4 %collective-permute-done.10 = bf16[3,1,320,512]{3,2,1,0:T(8,128)(2,1)S(1)} collective-permute-done((bf16[3,1,320,512]{3,2,1,0:T(8,128)(2,1)}, bf16[3,1,320,512]{3,2,1,0:T(8,128)(2,1)S(1)}, u32[]{:S(2)}, u32[]{:S(2)}) %collective-permute-start.10) | collective-permute-done | bytes 983072 | tf_op jit(solution)/shard_map/ppermute | solution.py:22
  196.3 2.8 pad_maximum_fusion.1
  199.1 27.2 %all-gather.7.cloned.1.call-done = bf16[1,1,2048,512]{3,2,1,0:T(8,128)(2,1)} async-done(((bf16[1,1,16,512]{3,2,1,0:T(8,128)(2,1)}), bf16[1,1,2048,512]{3,2,1,0:T(8,128)(2,1)}) %all-gather.7.cloned.1.call-update) | async-done | bytes 2097168 | tf_op jit(solution)/shard_map/all_gather | solution.py:55
  226.4 9.2 %fusion.4 = f32[4928,512]{1,0:T(8,128)} fusion(bf16[2048,512]{1,0:T(8,128)(2,1)} %bitcast.207, bf16[2880,512]{1,0:T(8,128)(2,1)} %bitcast.191, bf16[18,512,512]{2,1,0:T(8,128)(2,1)} %param.21), kind=kOutput, calls=%fused_computation.19 | convolution fusion | flops 2593783808 | bytes 15663104 | tf_op jit(solution)/shard_map/dot_general | solution.py:40
  235.5 12.5 %gather_fusion.4 = f32[2560,512]{1,0:T(8,128)} fusion(f32[4928,512]{1,0:T(8,128)} %fusion.4, s32[3072]{0:T(1024)S(1)} %pad_clamp_fusion.1), kind=kCustom, calls=%fused_computation.4 | custom fusion | bytes 10496000 | tf_op jit(solution)/shard_map/gather | solution.py:85
  248.1 11.0 %fusion.164 = (f32[2560]{0:T(1024)S(1)}, f32[2560,512]{0,1:T(8,128)}) fusion(bf16[8,512,512]{2,1,0:T(8,128)(2,1)} %param.22, f32[2560,512]{1,0:T(8,128)} %gather_fusion.5, f32[2560,512]{1,0:T(8,128)} %gather_fusion.4, bf16[2560,512]{0,1:T(8,128)(2,1)} %add_convert_fusion.1, bf16[18,512,512]{2,1,0:T(8,128)(2,1)} %param.21), kind=kOutput, calls=%fused_computation.220 | convolution fusion | flops 2694837760 | bytes 19408896 | tf_op jit(solution)/shard_map/dot_general | solution.py:32
  259.0 3.1 multiply_reduce_fusion
  262.1 5.3 %multiply_convert_fusion.22 = bf16[320,512]{1,0:T(8,128)(2,1)S(1)} fusion(f32[320,512]{1,0:T(8,128)S(1)} %fusion.80, bf16[2560,512]{0,1:T(8,128)(2,1)} %add_convert_fusion.1, f32[2560,512]{0,1:T(8,128)} %get-tuple-element.29, f32[512]{0:T(512)S(1)} %bitcast.204, f32[2560]{0:T(1024)S(1)} %add_rsqrt_fusion, f32[2560]{0:T(1024)S(1)} %broadcast_multiply_fusion, ...), kind=kOutput, calls=%fused_computation.82 | convolution fusion | flops 1016463360 | bytes 9404416 | tf_op jit(solution)/shard_map/dot_general | solution.py:40
  267.5 1.6 fusion.167
  269.8 2.7 collective-permute-start.13
  272.5 4.7 %collective-permute-done.12 = bf16[1,1,320,512]{3,2,1,0:T(8,128)(2,1)S(1)} collective-permute-done((bf16[1,1,320,512]{3,2,1,0:T(8,128)(2,1)S(1)}, bf16[1,1,320,512]{3,2,1,0:T(8,128)(2,1)S(1)}, u32[]{:S(2)}, u32[]{:S(2)}) %collective-permute-start.12) | collective-permute-done | bytes 327712 | tf_op jit(solution)/shard_map/ppermute | solution.py:22
  277.6 5.3 %collective-permute-start.15 = (bf16[3,1,320,512]{3,2,1,0:T(8,128)(2,1)S(1)}, bf16[3,1,320,512]{3,2,1,0:T(8,128)(2,1)S(1)}, u32[]{:S(2)}, u32[]{:S(2)}) collective-permute-start(bf16[3,1,320,512]{3,2,1,0:T(8,128)(2,1)S(1)} %pad_maximum_fusion.6), channel_id=1, source_target_pairs={{1,0},{2,1},{3,2},{4,3},{5,4},{6,5},{7,6},{8,7},{9,8},{10,9},{11,1... | collective-permute-start | bytes 2949128 | tf_op jit(solution)/shard_map/ppermute | solution.py:25
  283.0 3.1 fusion.67
  286.1 3.1 fusion.103
  289.2 14.6 %collective-permute-done.14 = bf16[3,1,320,512]{3,2,1,0:T(8,128)(2,1)S(1)} collective-permute-done((bf16[3,1,320,512]{3,2,1,0:T(8,128)(2,1)S(1)}, bf16[3,1,320,512]{3,2,1,0:T(8,128)(2,1)S(1)}, u32[]{:S(2)}, u32[]{:S(2)}) %collective-permute-start.14) | collective-permute-done | bytes 983072 | tf_op jit(solution)/shard_map/ppermute | solution.py:22
  304.2 5.3 %fusion.69 = f32[2880,512]{1,0:T(8,128)} fusion(bf16[2880,512]{1,0:T(8,128)(2,1)S(1)} %bitcast.179, bf16[18,512,512]{2,1,0:T(8,128)(2,1)} %param.21), kind=kOutput, calls=%fused_computation.96 | convolution fusion | flops 1509949440 | bytes 9371648 | tf_op jit(solution)/shard_map/dot_general | solution.py:40
  309.4 6.7 %gather_fusion.6 = f32[1024,512]{1,0:T(8,128)S(1)} fusion(f32[2880,512]{1,0:T(8,128)} %fusion.69, s32[1024]{0:T(1024)S(1)} %broadcast_clamp_fusion.2), kind=kCustom, calls=%fused_computation.6 | custom fusion | bytes 4198400 | tf_op jit(solution)/shard_map/gather | solution.py:114
  316.1 2.6 fusion.170
  320.0 6.7 %gather_fusion.7 = f32[1024,512]{1,0:T(8,128)S(1)} fusion(f32[2880,512]{1,0:T(8,128)} %fusion.69, s32[1024]{0:T(1024)S(1)} %get-tuple-element.43), kind=kCustom, calls=%fused_computation.7 | custom fusion | bytes 4198400 | tf_op jit(solution)/shard_map/gather | solution.py:114
  326.7 2.6 fusion.169
  329.6 1.1 copy-done.5
  330.6 6.7 %gather_fusion.8 = f32[1024,512]{1,0:T(8,128)S(1)} fusion(f32[2880,512]{1,0:T(8,128)} %fusion.69, s32[1024]{0:T(1024)S(1)} %get-tuple-element.42), kind=kCustom, calls=%fused_computation.8 | custom fusion | bytes 4198400 | tf_op jit(solution)/shard_map/gather | solution.py:114
  337.3 2.6 fusion.168
  340.2 1.0 copy-done.6
  341.3 5.7 %fusion.171 = (f32[1024]{0:T(1024)S(1)}, f32[1024,512]{1,0:T(8,128)S(1)}) fusion(bf16[8,512,512]{2,1,0:T(8,128)(2,1)} %param.22, f32[1024,512]{1,0:T(8,128)} %fusion.103, f32[1024,512]{0,1:T(8,128)} %copy-done.6, f32[1024,512]{0,1:T(8,128)} %copy-done.5, f32[1024,512]{0,1:T(8,128)} %copy-done.4, f32[1024]{0:T(1024)S(1)} %add_rsqrt_fusion.4, ...), kind=kOutput, calls=%fused_computation.225 | convolution fusion | flops 1082653696 | bytes 11565056 | tf_op jit(solution)/shard_map/dot_general | solution.py:32
  347.4 1.4 add_convert_fusion.3
  (106 shorter events, 9.8 us)
Async XLA Ops:
  6.5 10.0 %copy-start = (bf16[8,128,512]{2,1,0:T(8,128)(2,1)S(1)}, bf16[8,128,512]{2,1,0:T(8,128)(2,1)}, u32[]{:S(2)}) copy-start(bf16[8,128,512]{2,1,0:T(8,128)(2,1)} %param.12) | copy-start | bytes 3145732
  6.5 8.6 %copy-start.9 = (f32[8,512]{1,0:T(8,128)S(1)}, f32[8,512]{1,0:T(8,128)}, u32[]{:S(2)}) copy-start(f32[8,512]{1,0:T(8,128)} %param.23) | copy-start | bytes 49156
  6.5 9.2 %copy-start.13 = (s32[1,1,1536]{2,1,0:T(1,128)S(1)}, s32[1,1,1536]{2,1,0:T(1,128)}, u32[]{:S(2)}) copy-start(s32[1,1,1536]{2,1,0:T(1,128)} %param.15) | copy-start | bytes 18436
  6.5 9.2 %copy-start.8 = (s32[1,1,1536]{2,1,0:T(1,128)S(1)}, s32[1,1,1536]{2,1,0:T(1,128)}, u32[]{:S(2)}) copy-start(s32[1,1,1536]{2,1,0:T(1,128)} %param.16) | copy-start | bytes 18436
  6.5 106.8 %all-gather.5.cloned.1.call-start = ((), (), s32[]{:S(2)}) async-start(), calls=%async_computation | async-start | bytes 2113536 | tf_op jit(solution)/shard_map/all_gather | solution.py:55
  7.7 8.7 %collective-permute-start = (bf16[2,128,512]{2,1,0:T(8,128)(2,1)S(1)}, bf16[2,128,512]{2,1,0:T(8,128)(2,1)S(1)}, u32[]{:S(2)}, u32[]{:S(2)}) collective-permute-start(bf16[2,128,512]{2,1,0:T(8,128)(2,1)S(1)} %get-tuple-element.8), channel_id=1, source_target_pairs={{0,16},{16,32},{32,48},{48,64},{64,80},{80,96},{96,112},{112,0},{1... | collective-permute-start | bytes 786440 | tf_op jit(solution)/shard_map/ppermute | solution.py:22
  7.8 8.8 %collective-permute-start.1 = (bf16[2,128,512]{2,1,0:T(8,128)(2,1)S(1)}, bf16[2,128,512]{2,1,0:T(8,128)(2,1)S(1)}, u32[]{:S(2)}, u32[]{:S(2)}) collective-permute-start(bf16[2,128,512]{2,1,0:T(8,128)(2,1)S(1)} %get-tuple-element.7), channel_id=1, source_target_pairs={{16,0},{32,16},{48,32},{64,48},{80,64},{96,80},{112,96},{0,112},{1... | collective-permute-start | bytes 786440 | tf_op jit(solution)/shard_map/ppermute | solution.py:25
  16.7 10.4 %collective-permute-start.2 = (bf16[12,2,512]{2,1,0:T(2,128)(2,1)S(1)}, bf16[12,2,512]{2,1,0:T(2,128)(2,1)S(1)}, u32[]{:S(2)}, u32[]{:S(2)}) collective-permute-start(bf16[12,2,512]{2,1,0:T(2,128)(2,1)S(1)} %get-tuple-element.5), channel_id=1, source_target_pairs={{0,1},{1,2},{2,3},{3,4},{4,5},{5,6},{6,7},{7,8},{8,9},{9,10},{10,1... | collective-permute-start | bytes 73736 | tf_op jit(solution)/shard_map/ppermute | solution.py:22
  18.3 8.8 %collective-permute-start.3 = (bf16[12,2,512]{2,1,0:T(2,128)(2,1)S(1)}, bf16[12,2,512]{2,1,0:T(2,128)(2,1)S(1)}, u32[]{:S(2)}, u32[]{:S(2)}) collective-permute-start(bf16[12,2,512]{2,1,0:T(2,128)(2,1)S(1)} %get-tuple-element.6), channel_id=1, source_target_pairs={{1,0},{2,1},{3,2},{4,3},{5,4},{6,5},{7,6},{8,7},{9,8},{10,9},{11,1... | collective-permute-start | bytes 73736 | tf_op jit(solution)/shard_map/ppermute | solution.py:25
  41.5 5.1 %copy-start.3 = (bf16[1,1,320,512]{3,2,1,0:T(8,128)(2,1)S(1)}, bf16[1,1,320,512]{3,2,1,0:T(8,128)(2,1)}, u32[]{:S(2)}) copy-start(bf16[1,1,320,512]{3,2,1,0:T(8,128)(2,1)} %param.13) | copy-start | bytes 983044
  47.5 178.9 %all-gather.7.cloned.1.call-start = ((), (), s32[]{:S(2)}) async-start(), calls=%async_computation.1 | async-start | bytes 2113536 | tf_op jit(solution)/shard_map/all_gather | solution.py:55
  47.5 7.7 %collective-permute-start.4 = (bf16[1,1,320,512]{3,2,1,0:T(8,128)(2,1)S(1)}, bf16[1,1,320,512]{3,2,1,0:T(8,128)(2,1)S(1)}, u32[]{:S(2)}, u32[]{:S(2)}) collective-permute-start(bf16[1,1,320,512]{3,2,1,0:T(8,128)(2,1)S(1)} %bitcast.181), channel_id=1, source_target_pairs={{0,16},{16,32},{32,48},{48,64},{64,80},{80,96},{96,112},{112,0},{1... | collective-permute-start | bytes 983048 | tf_op jit(solution)/shard_map/ppermute | solution.py:22
  47.6 7.7 %collective-permute-start.5 = (bf16[1,1,320,512]{3,2,1,0:T(8,128)(2,1)S(1)}, bf16[1,1,320,512]{3,2,1,0:T(8,128)(2,1)S(1)}, u32[]{:S(2)}, u32[]{:S(2)}) collective-permute-start(bf16[1,1,320,512]{3,2,1,0:T(8,128)(2,1)S(1)} %bitcast.182), channel_id=1, source_target_pairs={{16,0},{32,16},{48,32},{64,48},{80,64},{96,80},{112,96},{0,112},{1... | collective-permute-start | bytes 983048 | tf_op jit(solution)/shard_map/ppermute | solution.py:25
  56.3 9.9 %copy-start.7 = (s32[1,1,2560]{2,1,0:T(1,128)S(1)}, s32[1,1,2560]{2,1,0:T(1,128)}, u32[]{:S(2)}) copy-start(s32[1,1,2560]{2,1,0:T(1,128)} %param.19) | copy-start | bytes 30724
  56.3 9.9 %copy-start.11 = (s32[1,1,2560]{2,1,0:T(1,128)S(1)}, s32[1,1,2560]{2,1,0:T(1,128)}, u32[]{:S(2)}) copy-start(s32[1,1,2560]{2,1,0:T(1,128)} %param.18) | copy-start | bytes 30724
  56.3 27.0 %collective-permute-start.6 = (bf16[3,1,320,512]{3,2,1,0:T(8,128)(2,1)}, bf16[3,1,320,512]{3,2,1,0:T(8,128)(2,1)S(1)}, u32[]{:S(2)}, u32[]{:S(2)}) collective-permute-start(bf16[3,1,320,512]{3,2,1,0:T(8,128)(2,1)} %pad_maximum_fusion.4), channel_id=1, source_target_pairs={{0,1},{1,2},{2,3},{3,4},{4,5},{5,6},{6,7},{7,8},{8,9},{9,10},{10,1... | collective-permute-start | bytes 2949128 | tf_op jit(solution)/shard_map/ppermute | solution.py:22
  56.3 27.0 %collective-permute-start.7 = (bf16[3,1,320,512]{3,2,1,0:T(8,128)(2,1)}, bf16[3,1,320,512]{3,2,1,0:T(8,128)(2,1)}, u32[]{:S(2)}, u32[]{:S(2)}) collective-permute-start(bf16[3,1,320,512]{3,2,1,0:T(8,128)(2,1)} %pad_maximum_fusion.4), channel_id=1, source_target_pairs={{1,0},{2,1},{3,2},{4,3},{5,4},{6,5},{7,6},{8,7},{9,8},{10,9},{11,1... | collective-permute-start | bytes 2949128 | tf_op jit(solution)/shard_map/ppermute | solution.py:25
  146.0 4.0 %copy-start.2 = (f32[2560,512]{0,1:T(8,128)S(1)}, f32[2560,512]{0,1:T(8,128)}, u32[]{:S(2)}) copy-start(f32[2560,512]{0,1:T(8,128)} %get-tuple-element.25) | copy-start | bytes 15728644
  157.8 16.9 %copy-start.10 = (s32[3,8,128]{2,1,0:T(8,128)S(1)}, s32[3,8,128]{2,1,0:T(8,128)}, u32[]{:S(2)}) copy-start(s32[3,8,128]{2,1,0:T(8,128)} %param.20) | copy-start | bytes 36868
  160.4 7.7 %collective-permute-start.8 = (bf16[1,1,320,512]{3,2,1,0:T(8,128)(2,1)S(1)}, bf16[1,1,320,512]{3,2,1,0:T(8,128)(2,1)S(1)}, u32[]{:S(2)}, u32[]{:S(2)}) collective-permute-start(bf16[1,1,320,512]{3,2,1,0:T(8,128)(2,1)S(1)} %bitcast.186), channel_id=1, source_target_pairs={{0,16},{16,32},{32,48},{48,64},{64,80},{80,96},{96,112},{112,0},{1... | collective-permute-start | bytes 983048 | tf_op jit(solution)/shard_map/ppermute | solution.py:22
  160.6 7.4 %collective-permute-start.9 = (bf16[1,1,320,512]{3,2,1,0:T(8,128)(2,1)S(1)}, bf16[1,1,320,512]{3,2,1,0:T(8,128)(2,1)S(1)}, u32[]{:S(2)}, u32[]{:S(2)}) collective-permute-start(bf16[1,1,320,512]{3,2,1,0:T(8,128)(2,1)S(1)} %bitcast.187), channel_id=1, source_target_pairs={{16,0},{32,16},{48,32},{64,48},{80,64},{96,80},{112,96},{0,112},{1... | collective-permute-start | bytes 983048 | tf_op jit(solution)/shard_map/ppermute | solution.py:25
  169.1 27.2 %collective-permute-start.10 = (bf16[3,1,320,512]{3,2,1,0:T(8,128)(2,1)}, bf16[3,1,320,512]{3,2,1,0:T(8,128)(2,1)S(1)}, u32[]{:S(2)}, u32[]{:S(2)}) collective-permute-start(bf16[3,1,320,512]{3,2,1,0:T(8,128)(2,1)} %pad_maximum_fusion.5), channel_id=1, source_target_pairs={{0,1},{1,2},{2,3},{3,4},{4,5},{5,6},{6,7},{7,8},{8,9},{9,10},{10,1... | collective-permute-start | bytes 2949128 | tf_op jit(solution)/shard_map/ppermute | solution.py:22
  169.6 26.8 %collective-permute-start.11 = (bf16[3,1,320,512]{3,2,1,0:T(8,128)(2,1)}, bf16[3,1,320,512]{3,2,1,0:T(8,128)(2,1)}, u32[]{:S(2)}, u32[]{:S(2)}) collective-permute-start(bf16[3,1,320,512]{3,2,1,0:T(8,128)(2,1)} %pad_maximum_fusion.5), channel_id=1, source_target_pairs={{1,0},{2,1},{3,2},{4,3},{5,4},{6,5},{7,6},{8,7},{9,8},{10,9},{11,1... | collective-permute-start | bytes 2949128 | tf_op jit(solution)/shard_map/ppermute | solution.py:25
  267.5 15.6 %copy-start.1 = (bf16[8,128,512]{2,1,0:T(8,128)(2,1)S(1)}, bf16[8,128,512]{2,1,0:T(8,128)(2,1)}, u32[]{:S(2)}) copy-start(bf16[8,128,512]{2,1,0:T(8,128)(2,1)} %param.12) | copy-start | bytes 3145732
  269.5 7.7 %collective-permute-start.12 = (bf16[1,1,320,512]{3,2,1,0:T(8,128)(2,1)S(1)}, bf16[1,1,320,512]{3,2,1,0:T(8,128)(2,1)S(1)}, u32[]{:S(2)}, u32[]{:S(2)}) collective-permute-start(bf16[1,1,320,512]{3,2,1,0:T(8,128)(2,1)S(1)} %fusion.136), channel_id=1, source_target_pairs={{0,16},{16,32},{32,48},{48,64},{64,80},{80,96},{96,112},{112,0},{1... | collective-permute-start | bytes 983048 | tf_op jit(solution)/shard_map/ppermute | solution.py:22
  269.8 7.4 %collective-permute-start.13 = (bf16[1,1,320,512]{3,2,1,0:T(8,128)(2,1)S(1)}, bf16[1,1,320,512]{3,2,1,0:T(8,128)(2,1)S(1)}, u32[]{:S(2)}, u32[]{:S(2)}) collective-permute-start(bf16[1,1,320,512]{3,2,1,0:T(8,128)(2,1)S(1)} %fusion.136), channel_id=1, source_target_pairs={{16,0},{32,16},{48,32},{64,48},{80,64},{96,80},{112,96},{0,112},{1... | collective-permute-start | bytes 983048 | tf_op jit(solution)/shard_map/ppermute | solution.py:25
  277.3 26.4 %collective-permute-start.14 = (bf16[3,1,320,512]{3,2,1,0:T(8,128)(2,1)S(1)}, bf16[3,1,320,512]{3,2,1,0:T(8,128)(2,1)S(1)}, u32[]{:S(2)}, u32[]{:S(2)}) collective-permute-start(bf16[3,1,320,512]{3,2,1,0:T(8,128)(2,1)S(1)} %pad_maximum_fusion.6), channel_id=1, source_target_pairs={{0,1},{1,2},{2,3},{3,4},{4,5},{5,6},{6,7},{7,8},{8,9},{9,10},{10,1... | collective-permute-start | bytes 2949128 | tf_op jit(solution)/shard_map/ppermute | solution.py:22
  277.6 26.1 %collective-permute-start.15 = (bf16[3,1,320,512]{3,2,1,0:T(8,128)(2,1)S(1)}, bf16[3,1,320,512]{3,2,1,0:T(8,128)(2,1)S(1)}, u32[]{:S(2)}, u32[]{:S(2)}) collective-permute-start(bf16[3,1,320,512]{3,2,1,0:T(8,128)(2,1)S(1)} %pad_maximum_fusion.6), channel_id=1, source_target_pairs={{1,0},{2,1},{3,2},{4,3},{5,4},{6,5},{7,6},{8,7},{9,8},{10,9},{11,1... | collective-permute-start | bytes 2949128 | tf_op jit(solution)/shard_map/ppermute | solution.py:25
  318.7 1.3 copy-start.4
  329.2 1.4 copy-start.5
  337.3 3.9 %copy-start.14 = (f32[1,512]{1,0:T(1,128)S(1)}, f32[1,512]{1,0:T(1,128)}, u32[]{:S(2)}) copy-start(f32[1,512]{1,0:T(1,128)} %get-tuple-element.16) | copy-start | bytes 6148
  339.9 1.4 copy-start.6
  341.3 6.1 %copy-start.12 = (f32[1,512]{1,0:T(1,128)S(1)}, f32[1,512]{1,0:T(1,128)}, u32[]{:S(2)}) copy-start(f32[1,512]{1,0:T(1,128)} %get-tuple-element.9) | copy-start | bytes 6148
Sparse Core Ops, SparseCore 0:
  47.6 65.7 all-gather.4
  160.5 65.8 all-gather.6
where the time goes:
time: 363 us; the launch traced here: 356 us
  waiting for transfers between devices  101 us (28%)
  matrix products  97.3 us (27%)
  local copies, waits for them, and re-layouts  83.3 us (23%)
  starting transfers between devices  34.7 us (10%)
  other arithmetic  24.4 us (7%)
  between operations  15 us (4%)
    all_gather x2, waiting for transfers between devices, coarse_rows(): return lax.all_gather(own_coarse, ('lat', 'lon'), axis=0, tiled=True)  54.5 us
    dot_general x15, matrix products, project(): return jnp.dot(rows_in, weight, preferred_element_type=jnp.float32)  53.4 us
    ppermute x8, waiting for transfers between devices, extended(): lax.ppermute(lax.slice_in_dim(block, block.shape[dim] - width, None, axis...  46.9 us
    dot_general x10, matrix products, finish(): result = jnp.dot(hidden, w_out, preferred_element_type=jnp.float32)  43.9 us
    ppermute x8, starting transfers between devices, extended(): lax.ppermute(lax.slice_in_dim(block, 0, width, axis=dim), axis, backward)  31.6 us
    gather x2, local copies, waits for them, and re-layouts, process(): sender_proj[senders]  25.1 us
    gather x3, local copies, waits for them, and re-layouts, decode(): sender_proj[corners[corner]] + own_proj  20.1 us
    gather x2, local copies, waits for them, and re-layouts, process(): project(mesh_own, weights_in[first_slot + 2])[targets]  15 us
  transfers between devices with their start and end apart: 18, of which 8 were waited for; matrix products, arithmetic and copies ran while one was open for 14% of the time, Pallas kernels for 0%

commit v1 on v0

v1 whole, which is shorter than its diff:
```python
import jax
import jax.numpy as jnp
from jax import lax
from jax.experimental import pallas as pl
from jax.experimental.pallas import tpu as pltpu
from jax.sharding import PartitionSpec as P

L = 512
ROWS = 8
COLS = 128
MESH = 320
BORDER = 64
COARSE = 16
EDGE = 2560
G2M = 1536
ROUNDS = 2
CELLS = ROWS * COLS
N_LAT = 8
N_LON = 16
OUT = 18

NORTH, SOUTH, STRIPS = 1024, 1280, 1536
GRID_ROWS = 1632
NEAR_AT, COARSE_AT, WIDE = 640, 1152, 3200
DEC_OWN, DEC_WIDE = 384, 896

TILE = 256
EPSILON = 1e-05
F32 = jnp.float32
BF16 = jnp.bfloat16
NEIGHBOURS = [(p, q) for p in (-1, 0, 1) for q in (-1, 0, 1) if (p, q) != (0, 0)]
PARTS = [(pl.ds(0, 256), "xyz"), (pl.ds(256, 256), "zxy")]


def dot(a, b):
    return jnp.dot(a, b, preferred_element_type=F32)


def hidden(before):
    half = 0.5 * before
    return (half + half * jnp.tanh(half)).astype(BF16)


def norm(result, gain):
    centre = jnp.sum(result, axis=-1, keepdims=True) * (1.0 / L)
    centred = result - centre
    spread = jnp.sum(centred * centred, axis=-1, keepdims=True) * (1.0 / L)
    return centred * lax.rsqrt(spread + EPSILON) * gain


def ones_where(mask):
    return jnp.where(mask, 1.0, 0.0).astype(BF16)


def steps_below(value, size, count):
    index = jnp.zeros_like(value)
    for step in range(1, count):
        index = index + jnp.where(value >= step * size, 1, 0)
    return index


def near_slot(source, own_at, near_at):
    block = steps_below(source, MESH, 9)
    row = source - block * MESH
    slot = block - jnp.where(block > 4, 1, 0)
    return jnp.where(block == 4, own_at + row, near_at + slot * BORDER + row)


def grid_slot(cell):
    r = steps_below(cell, COLS + 4, ROWS + 4)
    c = cell - r * (COLS + 4)
    north, south = r < 2, r >= ROWS + 2
    west, east = c < 2, c >= COLS + 2
    row = jnp.where(north, NORTH // COLS + r, jnp.where(south, SOUTH // COLS + r - (ROWS + 2), r - 2))
    inside = row * COLS + c - 2
    strip = jnp.where(north, 2, jnp.where(south, 4, 0)) + jnp.where(east, 1, 0)
    strip_row = jnp.where(north, r + ROWS - 2, jnp.where(south, r - (ROWS + 2), r - 2))
    strip_col = jnp.where(east, c - (COLS + 2), c)
    side = STRIPS + strip * 16 + strip_row * 2 + strip_col
    return jnp.where(west | east, side, inside)


def kernel(
    grid, mesh_in, edge_in, g2m_src, g2m_dst, g2m_count, mesh_src, mesh_dst, m2g_src,
    weights_in, weights_out, gains, out,
    w, cells, table, edges, acc, pick, place, coarse, near, proj, message, mesh_now, strips, square,
    local_sem, send_sem, recv_sem,
):
    lat, lon = lax.axis_index("lat"), lax.axis_index("lon")
    z, core = lax.div(lat, 2), lax.rem(lat, 2)
    x, y = lax.div(lon, 4), lax.rem(lon, 4)
    counts = {"local": 0, "remote": 0}

    def local(src, dst):
        i = counts["local"]
        counts["local"] += 1
        copy = pltpu.make_async_copy(src, dst, local_sem.at[i])
        copy.start()
        return copy

    def remote(src, dst, device):
        i = counts["remote"]
        counts["remote"] += 1
        copy = pltpu.make_async_remote_copy(
            src_ref=src, dst_ref=dst, send_sem=send_sem.at[i], recv_sem=recv_sem.at[i],
            device_id=device, device_id_type=pl.DeviceIdType.MESH,
        )
        copy.start()
        return copy

    def beside(p, q):
        return (lax.rem(lat + (p + N_LAT), N_LAT), lax.rem(lon + (q + N_LON), N_LON))

    def along(axis, d):
        if axis == "x":
            return (lat, lax.rem(x + d, 4) * 4 + y)
        if axis == "y":
            return (lat, x * 4 + lax.rem(y + d, 4))
        return (lax.rem(z + d, 4) * 2 + core, lon)

    sibling = (z * 2 + (1 - core), lon)

    got_grid = local(grid, cells.at[pl.ds(0, CELLS)])
    got_weights = []
    for first, many, first_out, many_out in ((0, 4, 0, 2), (4, 5, 2, 2), (9, 5, 4, 2), (14, 4, 6, 2)):
        got_weights.append((
            local(weights_in.at[pl.ds(first, many)], w.at[pl.ds(first, many)]),
            local(weights_out.at[pl.ds(first_out, many_out)], w.at[pl.ds(OUT + first_out, many_out)]),
        ))
        if first == 0:
            got_edges = local(edge_in, edges)

    barrier = pltpu.get_barrier_semaphore()
    peers = [beside(p, q) for p, q in NEIGHBOURS]
    peers += [along(axis, d) for axis in "xyz" for d in (1, 2, 3)] + [sibling]
    for peer in peers:
        pl.semaphore_signal(barrier, inc=1, device_id=peer, device_id_type=pl.DeviceIdType.MESH)
    pl.semaphore_wait(barrier, len(peers))

    halo = [
        remote(grid.at[pl.ds(CELLS - 256, 256)], cells.at[pl.ds(NORTH, 256)], beside(1, 0)),
        remote(grid.at[pl.ds(0, 256)], cells.at[pl.ds(SOUTH, 256)], beside(-1, 0)),
    ]
    got_grid.wait()
    i = lax.broadcasted_iota(jnp.int32, (16, COLS), 0)
    j = lax.broadcasted_iota(jnp.int32, (16, COLS), 1)
    for side, first, shift in ((0, COLS - 16, 14), (1, 0, 0)):
        rim = jnp.concatenate([cells[r * COLS + first : r * COLS + first + 16] for r in range(ROWS)], axis=0)
        wanted = (i >> 1) * 16 + shift + (i & 1)
        strips[side] = dot(ones_where(j == wanted), rim).astype(BF16)
    for side, q in ((0, 1), (1, -1)):
        for place_at, p in ((0, 0), (2, 1), (4, -1)):
            halo.append(remote(
                strips.at[side], cells.at[pl.ds(STRIPS + (place_at + side) * 16, 16)], beside(p, q)
            ))

    lanes = lax.broadcasted_iota(jnp.int32, (128, 128), 1).astype(F32)
    nodes = lax.broadcasted_iota(jnp.int32, (MESH, 128), 0)

    def columns(index, at):
        many = index.shape[0]
        square[...] = jnp.zeros_like(square)
        square[0:many] = index.astype(F32)
        turned = square[...].T
        for t in range(many):
            acc[t * 128 : t * 128 + 128, at : at + 128] = jnp.broadcast_to(turned[:, t : t + 1], (128, 128))

    live = g2m_count[...]
    lane = lax.broadcasted_iota(jnp.int32, (1, 128), 1)
    for t in range(G2M // 128):
        target = jnp.where(lane + t * 128 < live, g2m_dst[t : t + 1, :], -1)
        place[:, EDGE + t * 128 : EDGE + t * 128 + 128] = ones_where(nodes == target)
    for t in range(EDGE // 128):
        place[:, t * 128 : t * 128 + 128] = ones_where(nodes == mesh_dst[t : t + 1, :])

    columns(grid_slot(g2m_src[...]), 0)
    columns(g2m_dst[...] + GRID_ROWS, 128)

    @pl.loop(0, G2M // 128)
    def _(t):
        rows = pl.ds(pl.multiple_of(t * 128, 128), 128)
        first, second = acc[rows, 0:128], acc[rows, 128:256]
        for chunk in range(16):
            ids = lanes + float(chunk * 128)
            if chunk < 12:
                mask = first == ids
            elif chunk == 12:
                mask = (first == ids) | (second == ids)
            else:
                mask = second == ids
            pick[rows, chunk * 128 : chunk * 128 + 128] = ones_where(mask)

    got_weights[0][0].wait()
    got_weights[0][1].wait()

    @pl.loop(0, CELLS // TILE)
    def _(t):
        rows = pl.ds(pl.multiple_of(t * TILE, TILE), TILE)
        table[rows, :] = dot(cells[rows, :], w[0]).astype(BF16)

    table[GRID_ROWS : GRID_ROWS + MESH] = dot(mesh_in[...], w[1]).astype(BF16)
    table[GRID_ROWS + MESH :] = jnp.zeros((2048 - GRID_ROWS - MESH, L), BF16)
    for copy in halo:
        copy.wait_recv()
    table[CELLS:GRID_ROWS] = dot(cells[CELLS:GRID_ROWS], w[0]).astype(BF16)

    @pl.loop(0, G2M // TILE)
    def _(t):
        rows = pl.ds(pl.multiple_of(t * TILE, TILE), TILE)
        before = dot(pick[rows, 0:2048], table[...])
        message[rows, :] = norm(dot(hidden(before), w[OUT]), gains[0:1, :]).astype(BF16)

    def new_nodes(old, totals, first, k):
        before = dot(old, w[first]) + dot(totals.astype(BF16), w[first + 1])
        return (old.astype(F32) + norm(dot(hidden(before), w[OUT + k]), gains[k : k + 1, :])).astype(BF16)

    totals = dot(place[:, EDGE : EDGE + G2M], message[...])
    mesh_now[...] = new_nodes(mesh_in[...], totals, 2, 1)

    sent = list(halo)

    def send_near(r):
        copies = []
        for slot, (p, q) in enumerate(NEIGHBOURS):
            copies.append(remote(proj.at[r, pl.ds(0, BORDER)], near.at[r, slot], beside(-p, -q)))
        sent.extend(copies)
        return copies

    def block(r, part, known):
        at = {"x": x, "y": y, "z": z}
        for axis in known:
            at[axis] = slice(None)
        return coarse.at[r, at["z"], core, at["x"], at["y"], :, part]

    def stage(r, part, order, step):
        known = order[:step]
        ref = block(r, part, known)
        copies = [remote(ref, ref, along(order[step], d)) for d in (1, 2, 3)]
        sent.extend(copies)
        return copies

    def arrived(r, part, order, d):
        at = {"x": x, "y": y, "z": z}
        at[order[2]] = lax.rem(at[order[2]] + (4 - d), 4)
        for axis in order[:2]:
            at[axis] = slice(None)
        return coarse.at[r, at["z"], core, at["x"], at["y"], :, part]

    for r in range(ROUNDS):
        first = 4 + 5 * r
        got_weights[1 + r][0].wait()
        got_weights[1 + r][1].wait()
        sender = dot(mesh_now[...], w[first + 1]).astype(BF16)
        proj[r, 0:MESH] = sender
        coarse[r, z, core, x, y] = sender[MESH - COARSE :]
        moving = [stage(r, part, order, 0) for part, order in PARTS]
        got_near = send_near(r)
        proj[r, MESH : 2 * MESH] = dot(mesh_now[...], w[first + 2]).astype(BF16)

        def wait_stage(step):
            for k, (part, order) in enumerate(PARTS):
                for copy in moving[k]:
                    copy.wait_recv()
                moving[k] = stage(r, part, order, step)

        if r == 0:
            got_edges.wait()
            source = mesh_src[...]
            slot = jnp.where(source >= 9 * MESH, COARSE_AT - 9 * MESH + source, near_slot(source, 0, NEAR_AT))
            columns(slot, 0)
            columns(mesh_dst[...] + MESH, 128)

            @pl.loop(0, EDGE // 128)
            def _(t):
                rows = pl.ds(pl.multiple_of(t * 128, 128), 128)
                one, two = acc[rows, 0:128], acc[rows, 128:256]
                for chunk in range(WIDE // 128):
                    ids = lanes + float(chunk * 128)
                    if chunk in (3, 4):
                        mask = two == ids
                    elif chunk == 2:
                        mask = (one == ids) | (two == ids)
                    else:
                        mask = one == ids
                    pick[rows, chunk * 128 : chunk * 128 + 128] = ones_where(mask)

        wait_stage(1)

        def own_part(t):
            rows = pl.ds(pl.multiple_of(t * TILE, TILE), TILE)
            acc[rows, :] = dot(edges[rows, :], w[first]) + dot(pick[rows, 0:NEAR_AT], proj[r])

        pl.loop(0, 5)(own_part)
        wait_stage(2)
        across = []
        for part, order in PARTS:
            ref = block(r, part, order[:2])
            across.append(remote(ref, ref, sibling))
        pl.loop(5, 10)(own_part)
        for copy in got_near:
            copy.wait_recv()

        @pl.loop(0, EDGE // TILE)
        def _(t):
            rows = pl.ds(pl.multiple_of(t * TILE, TILE), TILE)
            acc[rows, :] += dot(pick[rows, NEAR_AT:COARSE_AT], near[r].reshape(8 * BORDER, L))

        for d in (1, 2, 3):
            for k, (part, order) in enumerate(PARTS):
                moving[k][d - 1].wait_recv()
                ref = arrived(r, part, order, d)
                across.append(remote(ref, ref, sibling))
        sent.extend(across)
        for copy in across:
            copy.wait_recv()

        @pl.loop(0, EDGE // TILE)
        def _(t):
            rows = pl.ds(pl.multiple_of(t * TILE, TILE), TILE)
            before = acc[rows, :] + dot(pick[rows, COARSE_AT:WIDE], coarse[r].reshape(2048, L))
            update = norm(dot(hidden(before), w[OUT + 2 + 2 * r]), gains[2 + 2 * r : 3 + 2 * r, :])
            edges[rows, :] = (edges[rows, :].astype(F32) + update).astype(BF16)

        totals = dot(place[:, 0:EDGE], edges[...])
        mesh_now[...] = new_nodes(mesh_now[...], totals, first + 3, 3 + 2 * r)

    got_weights[3][0].wait()
    got_weights[3][1].wait()
    proj[ROUNDS, 0:MESH] = dot(mesh_now[...], w[14]).astype(BF16)
    got_near = send_near(ROUNDS)
    proj[ROUNDS, MESH : 2 * MESH] = jnp.zeros((MESH, L), BF16)

    columns(near_slot(m2g_src[...], 0, DEC_OWN), 0)

    @pl.loop(0, ROWS)
    def _(t):
        to = pl.ds(pl.multiple_of(t * 128, 128), 128)
        for corner in range(3):
            one = acc[pl.ds(pl.multiple_of(corner * CELLS + t * 128, 128), 128), 0:128]
            for chunk in range(DEC_WIDE // 128):
                at = corner * DEC_WIDE + chunk * 128
                pick[to, at : at + 128] = ones_where(one == lanes + float(chunk * 128))

    @pl.loop(0, CELLS // TILE)
    def _(t):
        rows = pl.ds(pl.multiple_of(t * TILE, TILE), TILE)
        base = dot(cells[rows, :], w[15])
        for corner in range(3):
            at = corner * DEC_WIDE
            to = pl.ds(pl.multiple_of(corner * CELLS + t * TILE, TILE), TILE)
            acc[to, :] = base + dot(pick[rows, at : at + DEC_OWN], proj[ROUNDS, 0:DEC_OWN])

    for copy in got_near:
        copy.wait_recv()

    @pl.loop(0, CELLS // TILE)
    def _(t):
        rows = pl.ds(pl.multiple_of(t * TILE, TILE), TILE)
        totals = jnp.zeros((TILE, L), F32)
        for corner in range(3):
            at = corner * DEC_WIDE
            to = pl.ds(pl.multiple_of(corner * CELLS + t * TILE, TILE), TILE)
            before = acc[to, :] + dot(
                pick[rows, at + DEC_OWN : at + DEC_WIDE], near[ROUNDS].reshape(8 * BORDER, L)
            )
            totals = totals + norm(dot(hidden(before), w[OUT + 6]), gains[6:7, :])
        out[rows, :] = new_nodes(cells[rows, :], totals, 16, 7)

    for copy in sent:
        copy.wait_send()


def on_device(
    grid_latent, mesh_latent, edge_latent, g2m_src, g2m_dst, g2m_count, mesh_src, mesh_dst, m2g_src,
    weights_in, weights_out, gains,
):
    anywhere = pl.BlockSpec(memory_space=pl.ANY)
    vmem = pl.BlockSpec(memory_space=pltpu.VMEM)
    result = pl.pallas_call(
        kernel,
        out_shape=jax.ShapeDtypeStruct((CELLS, L), BF16),
        in_specs=[anywhere, vmem, anywhere] + [vmem] * 6 + [anywhere, anywhere, vmem],
        out_specs=vmem,
        scratch_shapes=[
            pltpu.VMEM((26, L, L), BF16),
            pltpu.VMEM((GRID_ROWS, L), BF16),
            pltpu.VMEM((2048, L), BF16),
            pltpu.VMEM((EDGE, L), BF16),
            pltpu.VMEM((3 * CELLS, L), F32),
            pltpu.VMEM((EDGE, WIDE), BF16),
            pltpu.VMEM((MESH, EDGE + G2M), BF16),
            pltpu.VMEM((ROUNDS, 4, 2, 4, 4, COARSE, L), BF16),
            pltpu.VMEM((ROUNDS + 1, 8, BORDER, L), BF16),
            pltpu.VMEM((ROUNDS + 1, 2 * MESH, L), BF16),
            pltpu.VMEM((G2M, L), BF16),
            pltpu.VMEM((MESH, L), BF16),
            pltpu.VMEM((2, 16, L), BF16),
            pltpu.VMEM((128, 128), F32),
            pltpu.SemaphoreType.DMA((10,)),
            pltpu.SemaphoreType.DMA((84,)),
            pltpu.SemaphoreType.DMA((84,)),
        ],
        compiler_params=pltpu.CompilerParams(
            collective_id=0, has_side_effects=True, vmem_limit_bytes=62 * 1024 * 1024
        ),
        cost_estimate=pl.CostEstimate(flops=40_000_000_000, bytes_accessed=20_000_000, transcendentals=10_000_000),
    )(
        grid_latent.reshape(CELLS, L), mesh_latent.reshape(MESH, L), edge_latent.reshape(EDGE, L),
        g2m_src.reshape(-1, 128), g2m_dst.reshape(-1, 128), g2m_count,
        mesh_src.reshape(-1, 128), mesh_dst.reshape(-1, 128), m2g_src.reshape(-1, 128),
        weights_in, weights_out, gains,
    )
    return result.reshape(grid_latent.shape)


def solution(mesh):
    placed = (
        P("lat", "lon", None),
        P("lat", "lon", None, None),
        P("lat", "lon", None, None),
        P("lat", "lon", None),
        P("lat", "lon", None),
        P("lat", "lon"),
        P("lat", "lon", None),
        P("lat", "lon", None),
        P(None, "lat", "lon"),
        P(),
        P(),
        P(),
    )
    return jax.shard_map(
        on_device, mesh=mesh, in_specs=placed, out_specs=P("lat", "lon", None), check_vma=False
    )
```

time: 363 us -> 118 us (0.33); the launches traced: 356 us -> 118 us
  Pallas kernels: 0 us -> 109 us
  waiting for transfers between devices: 101 us -> 0 us
  matrix products: 97.3 us -> 0 us
  local copies, waits for them, and re-layouts: 83.3 us -> 2.26 us
  starting transfers between devices: 34.7 us -> 0 us
  other arithmetic: 24.4 us -> 5.27 us
  between operations: 15 us -> 0.66 us
    pallas_call x0 -> x1, Pallas kernels: none -> 109 us  [on_device(): pl.pallas_call(kernel, out_shape=jax.ShapeDtypeStruct((CELLS, L), BF16),...]
    dot_general x25 -> x0, matrix products: 97.3 us -> none  [the longest x15 53.4 us: project(): return jnp.dot(rows_in, weight, preferred_element_type=jnp.float32)]
    gather x9 -> x0, local copies, waits for them, and re-layouts: 70 us -> none  [the longest x2 25.1 us: process(): sender_proj[senders]]
    all_gather x2 -> x0, waiting for transfers between devices: 54.5 us -> none  [coarse_rows(): return lax.all_gather(own_coarse, ('lat', 'lon'), axis=0, tiled=True)]
    ppermute x16 -> x0, waiting for transfers between devices: 46.9 us -> none  [the longest x8 46.9 us: extended(): lax.ppermute(lax.slice_in_dim(block, block.shape[dim] - width, None, axis...]
    ppermute x16 -> x0, starting transfers between devices: 34.6 us -> none  [the longest x8 31.6 us: extended(): lax.ppermute(lax.slice_in_dim(block, 0, width, axis=dim), axis, backward)]
    concatenate x7 -> x0, other arithmetic: 8.77 us -> none  [extended(): block = jnp.concatenate([low, block, high], axis=dim)]
    reduce_sum x10 -> x0, other arithmetic: 8.72 us -> none  [finish(): spread = jnp.mean(centred * centred, axis=-1, keepdims=True)]
  transfers between devices with their start and end apart: 18 -> 0, of which waited for: 8 -> 0; matrix products, arithmetic and copies ran while one was open for 14% -> 0% of each run, Pallas kernels for 0% -> 0%
where the time goes in v1:
time: 118 us
  Pallas kernels  109 us (92%)
  other arithmetic  5.27 us (4%)
  local copies, waits for them, and re-layouts  2.26 us (2%)
    pallas_call x1, Pallas kernels, on_device(): pl.pallas_call(kernel, out_shape=jax.ShapeDtypeStruct((CELLS, L), BF16),...  109 us
    unnamed x4, other arithmetic  5.27 us

profile of v1, /device:TPU:0, one launch (start us, length us, event | category | flops | bytes accessed | tf_op | source)
XLA Modules:
  0.0 117.6 jit_solution(14711657800168243236)
XLA Ops:
  0.7 1.3 %reduce = s32[1536]{0:T(1024)} reduce(s32[1,1,1536]{2,1,0:T(1,128)} %param.15, s32[]{:T(128)} %constant.7), dimensions={0,1}, to_apply=%param.15.reduce_sub_computation | reduce | bytes 12292 | tf_op args[3]
  2.0 1.3 %reduce.1 = s32[1536]{0:T(1024)} reduce(s32[1,1,1536]{2,1,0:T(1,128)} %param.16, s32[]{:T(128)} %constant.7), dimensions={0,1}, to_apply=%param.16.reduce_sub_computation | reduce | bytes 12292 | tf_op args[4]
  3.3 1.3 %reduce.2 = s32[2560]{0:T(1024)} reduce(s32[1,1,2560]{2,1,0:T(1,128)} %param.18, s32[]{:T(128)} %constant.7), dimensions={0,1}, to_apply=%param.18.reduce_sub_computation | reduce | bytes 20484 | tf_op args[6]
  4.6 1.3 %reduce.3 = s32[2560]{0:T(1024)} reduce(s32[1,1,2560]{2,1,0:T(1,128)} %param.19, s32[]{:T(128)} %constant.7), dimensions={0,1}, to_apply=%param.19.reduce_sub_computation | reduce | bytes 20484 | tf_op args[7]
  5.9 109.4 %shard_map.118 = bf16[1024,512]{1,0:T(8,128)(2,1)} custom-call(bf16[1024,512]{1,0:T(8,128)(2,1)} %bitcast.15, bf16[320,512]{1,0:T(8,128)(2,1)} %bitcast.16, bf16[2560,512]{1,0:T(8,128)(2,1)} %bitcast.14, s32[12,128]{1,0:T(8,128)} %bitcast.12, s32[12,128]{1,0:T(8,128)} %bitcast.13, s32[1,1]{1,0:T(1,128)S(6)} %copy.14.g2m_count, s32[20,128]{1,0:T(8,128)} %bitcast.10, ...), custom_call_target="tpu_custom_call" | custom-call | flops 40000000000 | bytes 20000000 | tf_op jit(solution)/shard_map/pallas_call | solution.py:379
  115.4 2.3 %copy.15 = bf16[8,128,512]{2,1,0:T(8,128)(2,1)} copy(bf16[8,128,512]{2,1,0:T(8,128)(2,1)} %bitcast.9) | data formatting | bytes 2097152

commit v2 on v1

v2 whole, which is shorter than its diff:
```python
import jax
import jax.numpy as jnp
from jax import lax
from jax.experimental import pallas as pl
from jax.experimental.pallas import tpu as pltpu
from jax.sharding import PartitionSpec as P

L = 512
ROWS = 8
COLS = 128
MESH = 320
BORDER = 64
COARSE = 16
EDGE = 2560
G2M = 1536
ROUNDS = 2
CELLS = ROWS * COLS
N_LAT = 8
N_LON = 16
OUT = 18

NORTH, SOUTH, STRIPS = 1408, 1664, 1920
GRID_ROWS = 1632
NEAR_AT, COARSE_AT, WIDE = 640, 1152, 3200
DEC_OWN, DEC_WIDE = 384, 896

TILE = 512
EPSILON = 1e-05
F32 = jnp.float32
BF16 = jnp.bfloat16
NEIGHBOURS = [(p, q) for p in (-1, 0, 1) for q in (-1, 0, 1) if (p, q) != (0, 0)]
XY = [(i, j, 0) for i in range(4) for j in range(4) if (i, j) != (0, 0)]
YZ = [(0, i, j) for i in range(4) for j in range(4) if (i, j) != (0, 0)]
PARTS = [(pl.ds(0, 256), "z", XY), (pl.ds(256, 256), "x", YZ)]


def dot(a, b):
    return jnp.dot(a, b, preferred_element_type=F32)


def hidden(before):
    half = 0.5 * before
    return (half + half * jnp.tanh(half)).astype(BF16)


def norm(result, gain):
    centre = jnp.sum(result, axis=-1, keepdims=True) * (1.0 / L)
    centred = result - centre
    spread = jnp.sum(centred * centred, axis=-1, keepdims=True) * (1.0 / L)
    return centred * lax.rsqrt(spread + EPSILON) * gain


def ones_where(mask):
    return jnp.where(mask, 1.0, 0.0).astype(BF16)


def steps_below(value, size, count):
    index = jnp.zeros_like(value)
    for step in range(1, count):
        index = index + jnp.where(value >= step * size, 1, 0)
    return index


def near_slot(source, own_at, near_at):
    block = steps_below(source, MESH, 9)
    row = source - block * MESH
    slot = block - jnp.where(block > 4, 1, 0)
    return jnp.where(block == 4, own_at + row, near_at + slot * BORDER + row)


def grid_slot(cell):
    r = steps_below(cell, COLS + 4, ROWS + 4)
    c = cell - r * (COLS + 4)
    north, south = r < 2, r >= ROWS + 2
    west, east = c < 2, c >= COLS + 2
    inside = (r - 2) * COLS + c - 2
    inside = jnp.where(north, NORTH + r * COLS + c - 2, inside)
    inside = jnp.where(south, SOUTH + (r - (ROWS + 2)) * COLS + c - 2, inside)
    strip = jnp.where(north, 2, jnp.where(south, 4, 0)) + jnp.where(east, 1, 0)
    strip_row = jnp.where(north, r + ROWS - 2, jnp.where(south, r - (ROWS + 2), r - 2))
    strip_col = jnp.where(east, c - (COLS + 2), c)
    side = STRIPS + strip * 16 + strip_row * 2 + strip_col
    return jnp.where(west | east, side, inside)


def edge_slot(source, core):
    far = source - 9 * MESH
    other = ((far >> 8) + core) & 1
    coarse = COARSE_AT + other * 1024 + (far >> 9) * 256 + (far & 255)
    return jnp.where(far >= 0, coarse, near_slot(source, 0, NEAR_AT))


def kernel(
    grid, mesh_in, edge_in, g2m_src, g2m_dst, g2m_count, mesh_src, mesh_dst, m2g_src,
    weights_in, weights_out, gains, out,
    w, cells, table, edges, acc, pick, place, coarse, near, proj, message, mesh_now, own_part, strips, square,
    local_sem, send_sem, recv_sem,
):
    lat, lon = lax.axis_index("lat"), lax.axis_index("lon")
    z, core = lax.div(lat, 2), lax.rem(lat, 2)
    x, y = lax.div(lon, 4), lax.rem(lon, 4)
    counts = {"local": 0, "remote": 0}

    def local(src, dst):
        i = counts["local"]
        counts["local"] += 1
        copy = pltpu.make_async_copy(src, dst, local_sem.at[i])
        copy.start()
        return copy

    def remote(src, dst, device):
        i = counts["remote"]
        counts["remote"] += 1
        copy = pltpu.make_async_remote_copy(
            src_ref=src, dst_ref=dst, send_sem=send_sem.at[i], recv_sem=recv_sem.at[i],
            device_id=device, device_id_type=pl.DeviceIdType.MESH,
        )
        copy.start()
        return copy

    def beside(p, q):
        return (lax.rem(lat + (p + N_LAT), N_LAT), lax.rem(lon + (q + N_LON), N_LON))

    def chip(dx, dy, dz):
        return (lax.rem(z + dz, 4) * 2 + core, lax.rem(x + dx, 4) * 4 + lax.rem(y + dy, 4))

    sibling = (z * 2 + (1 - core), lon)

    got_grid = local(grid, cells.at[pl.ds(0, CELLS)])
    got_weights = []
    for first, many, first_out, many_out in ((0, 4, 0, 2), (4, 5, 2, 2), (9, 5, 4, 2), (14, 4, 6, 2)):
        got_weights.append((
            local(weights_in.at[pl.ds(first, many)], w.at[pl.ds(first, many)]),
            local(weights_out.at[pl.ds(first_out, many_out)], w.at[pl.ds(OUT + first_out, many_out)]),
        ))
        if first == 0:
            got_edges = local(edge_in, edges)

    barrier = pltpu.get_barrier_semaphore()
    peers = [beside(p, q) for p, q in NEIGHBOURS] + [chip(*d) for d in sorted(set(XY + YZ))] + [sibling]
    for peer in peers:
        pl.semaphore_signal(barrier, inc=1, device_id=peer, device_id_type=pl.DeviceIdType.MESH)

    got_grid.wait()
    i = lax.broadcasted_iota(jnp.int32, (16, COLS), 0)
    j = lax.broadcasted_iota(jnp.int32, (16, COLS), 1)
    for side, first, shift in ((0, COLS - 16, 14), (1, 0, 0)):
        rim = jnp.concatenate([cells[r * COLS + first : r * COLS + first + 16] for r in range(ROWS)], axis=0)
        wanted = (i >> 1) * 16 + shift + (i & 1)
        strips[side] = dot(ones_where(j == wanted), rim).astype(BF16)

    pl.semaphore_wait(barrier, len(peers))
    halo = [
        remote(grid.at[pl.ds(CELLS - 256, 256)], cells.at[pl.ds(CELLS, 256)], beside(1, 0)),
        remote(grid.at[pl.ds(0, 256)], cells.at[pl.ds(CELLS + 256, 256)], beside(-1, 0)),
    ]
    for side, q in ((0, 1), (1, -1)):
        for place_at, p in ((0, 0), (2, 1), (4, -1)):
            to = CELLS + 512 + (place_at + side) * 16
            halo.append(remote(strips.at[side], cells.at[pl.ds(to, 16)], beside(p, q)))

    lanes = lax.broadcasted_iota(jnp.int32, (128, 128), 1).astype(F32)
    nodes = lax.broadcasted_iota(jnp.int32, (MESH, 128), 0)

    def stacked(ref):
        square[...] = jnp.zeros_like(square)
        many = ref.shape[1] // 128
        for t in range(many):
            square[t : t + 1, :] = ref[0:1, t * 128 : t * 128 + 128].astype(F32)
        return square[...].astype(jnp.int32), many

    def columns(index, many, at):
        turned = index.astype(F32).T
        for t in range(many):
            acc[t * 128 : t * 128 + 128, at : at + 128] = jnp.broadcast_to(turned[:, t : t + 1], (128, 128))

    source, many = stacked(g2m_src)
    columns(grid_slot(source), many, 0)
    target, many = stacked(g2m_dst)
    columns(target + CELLS, many, 128)

    @pl.loop(0, G2M // 128)
    def _(t):
        rows = pl.ds(pl.multiple_of(t * 128, 128), 128)
        first, second = acc[rows, 0:128], acc[rows, 128:256]
        for chunk in range(16):
            ids = lanes + float(chunk * 128)
            mask = (second if 8 <= chunk < 11 else first) == ids
            pick[rows, chunk * 128 : chunk * 128 + 128] = ones_where(mask)

    live = g2m_count[...]
    lane = lax.broadcasted_iota(jnp.int32, (1, 128), 1)
    for t in range(G2M // 128):
        target = jnp.where(lane + t * 128 < live, g2m_dst[0:1, t * 128 : t * 128 + 128], -1)
        place[:, EDGE + t * 128 : EDGE + t * 128 + 128] = ones_where(nodes == target)

    got_weights[0][0].wait()
    got_weights[0][1].wait()

    @pl.loop(0, CELLS // TILE)
    def _(t):
        rows = pl.ds(pl.multiple_of(t * TILE, TILE), TILE)
        table[rows, :] = dot(cells[rows, :], w[0]).astype(BF16)

    table[CELLS : CELLS + MESH] = dot(mesh_in[...], w[1]).astype(BF16)
    table[CELLS + MESH : NORTH] = jnp.zeros((NORTH - CELLS - MESH, L), BF16)
    table[NORTH + 608 :] = jnp.zeros((2048 - NORTH - 608, L), BF16)
    own_part[...] = dot(mesh_in[...], w[2])

    @pl.loop(0, G2M // TILE)
    def _(t):
        rows = pl.ds(pl.multiple_of(t * TILE, TILE), TILE)
        acc[rows, :] = dot(pick[rows, 0:NORTH], table[0:NORTH])

    for copy in halo:
        copy.wait_recv()
    table[NORTH : NORTH + 608] = dot(cells[CELLS:GRID_ROWS], w[0]).astype(BF16)

    @pl.loop(0, G2M // TILE)
    def _(t):
        rows = pl.ds(pl.multiple_of(t * TILE, TILE), TILE)
        before = acc[rows, :] + dot(pick[rows, NORTH:2048], table[NORTH:2048])
        message[rows, :] = norm(dot(hidden(before), w[OUT]), gains[0:1, :]).astype(BF16)

    def new_nodes(old, self_part, totals, second, k):
        before = self_part + dot(totals.astype(BF16), w[second])
        return (old.astype(F32) + norm(dot(hidden(before), w[OUT + k]), gains[k : k + 1, :])).astype(BF16)

    def update_encoded(a, b):
        totals = dot(place[a:b, EDGE : EDGE + G2M], message[...])
        mesh_now[a:b] = new_nodes(mesh_in[a:b], own_part[a:b], totals, 3, 1)

    def update_round(r):
        def update(a, b):
            totals = dot(place[a:b, 0:EDGE], edges[...])
            mesh_now[a:b] = new_nodes(mesh_now[a:b], own_part[a:b], totals, 8 + 5 * r, 3 + 2 * r)

        return update

    sent = list(halo)

    def send_near(r):
        copies = []
        for slot, (p, q) in enumerate(NEIGHBOURS):
            copies.append(remote(proj.at[r, pl.ds(0, BORDER)], near.at[r, slot], beside(-p, -q)))
        sent.extend(copies)
        return copies

    def plane(r, part, axis, d):
        here = lax.rem({"x": x, "z": z}[axis] + (4 - d), 4)
        if axis == "z":
            return coarse.at[r, 0, here, :, :, :, part]
        return coarse.at[r, 0, :, here, :, :, part]

    update = update_encoded
    for r in range(ROUNDS):
        first = 4 + 5 * r
        got_weights[1 + r][0].wait()
        got_weights[1 + r][1].wait()
        update(MESH - COARSE, MESH)
        coarse[r, 0, z, x, y] = dot(mesh_now[MESH - COARSE : MESH], w[first + 1]).astype(BF16)
        arriving = []
        for part, axis, offsets in PARTS:
            ref = coarse.at[r, 0, z, x, y, :, part]
            arriving.append([remote(ref, ref, chip(*d)) for d in offsets])
            sent.extend(arriving[-1])
        update(0, MESH - COARSE)
        proj[r, 0:MESH] = dot(mesh_now[...], w[first + 1]).astype(BF16)
        got_near = send_near(r)
        proj[r, MESH : 2 * MESH] = dot(mesh_now[...], w[first + 2]).astype(BF16)
        own_part[...] = dot(mesh_now[...], w[first + 3])

        if r == 0:
            got_edges.wait()
            source, many = stacked(mesh_src)
            columns(edge_slot(source, core), many, 0)
            target, many = stacked(mesh_dst)
            columns(target + MESH, many, 128)

        across = []

        def second_stage():
            moving = []
            for k, (part, axis, offsets) in enumerate(PARTS):
                for copy in arriving[k]:
                    copy.wait_recv()
                ref = plane(r, part, axis, 0)
                moving.append([
                    remote(ref, ref, chip(**{"dx": 0, "dy": 0, "dz": 0, "d" + axis: d})) for d in (1, 2, 3)
                ])
                sent.extend(moving[-1])
            for part, axis, offsets in PARTS:
                across.append(forward(part, axis, 0))
            return moving

        def forward(part, axis, d):
            here = lax.rem({"x": x, "z": z}[axis] + (4 - d), 4)
            if axis == "z":
                return remote(
                    coarse.at[r, 0, here, :, :, :, part], coarse.at[r, 1, here, :, :, :, part], sibling
                )
            return remote(
                coarse.at[r, 0, :, here, :, :, part], coarse.at[r, 1, :, here, :, :, part], sibling
            )

        if r == 0:

            @pl.loop(0, EDGE // 128)
            def _(t):
                rows = pl.ds(pl.multiple_of(t * 128, 128), 128)
                one, two = acc[rows, 0:128], acc[rows, 128:256]
                for chunk in range(WIDE // 128):
                    ids = lanes + float(chunk * 128)
                    if chunk in (3, 4):
                        mask = two == ids
                    elif chunk == 2:
                        mask = (one == ids) | (two == ids)
                    else:
                        mask = one == ids
                    pick[rows, chunk * 128 : chunk * 128 + 128] = ones_where(mask)

            moving = second_stage()
            for t in range(EDGE // 128):
                place[:, t * 128 : t * 128 + 128] = ones_where(nodes == mesh_dst[0:1, t * 128 : t * 128 + 128])

        @pl.loop(0, EDGE // TILE)
        def _(t):
            rows = pl.ds(pl.multiple_of(t * TILE, TILE), TILE)
            acc[rows, :] = dot(edges[rows, :], w[first]) + dot(pick[rows, 0:NEAR_AT], proj[r])

        if r > 0:
            moving = second_stage()
        for copy in got_near:
            copy.wait_recv()

        @pl.loop(0, EDGE // TILE)
        def _(t):
            rows = pl.ds(pl.multiple_of(t * TILE, TILE), TILE)
            acc[rows, :] += dot(pick[rows, NEAR_AT:COARSE_AT], near[r].reshape(8 * BORDER, L))

        for d in (1, 2, 3):
            for k, (part, axis, offsets) in enumerate(PARTS):
                moving[k][d - 1].wait_recv()
                across.append(forward(part, axis, d))
        sent.extend(across)

        @pl.loop(0, EDGE // TILE)
        def _(t):
            rows = pl.ds(pl.multiple_of(t * TILE, TILE), TILE)
            acc[rows, :] += dot(pick[rows, COARSE_AT : COARSE_AT + 1024], coarse[r, 0].reshape(1024, L))

        for copy in across:
            copy.wait_recv()

        @pl.loop(0, EDGE // TILE)
        def _(t):
            rows = pl.ds(pl.multiple_of(t * TILE, TILE), TILE)
            before = acc[rows, :] + dot(pick[rows, COARSE_AT + 1024 : WIDE], coarse[r, 1].reshape(1024, L))
            result = norm(dot(hidden(before), w[OUT + 2 + 2 * r]), gains[2 + 2 * r : 3 + 2 * r, :])
            edges[rows, :] = (edges[rows, :].astype(F32) + result).astype(BF16)

        update = update_round(r)

    got_weights[3][0].wait()
    got_weights[3][1].wait()
    update(0, BORDER)
    proj[ROUNDS, 0:BORDER] = dot(mesh_now[0:BORDER], w[14]).astype(BF16)
    got_near = send_near(ROUNDS)
    update(BORDER, MESH)
    proj[ROUNDS, BORDER:MESH] = dot(mesh_now[BORDER:MESH], w[14]).astype(BF16)
    proj[ROUNDS, MESH : 2 * MESH] = jnp.zeros((MESH, L), BF16)

    square[...] = jnp.zeros_like(square)
    square[0:24] = m2g_src[...].astype(F32)
    columns(near_slot(square[...].astype(jnp.int32), 0, DEC_OWN), 24, 0)

    @pl.loop(0, ROWS)
    def _(t):
        to = pl.ds(pl.multiple_of(t * 128, 128), 128)
        for corner in range(3):
            one = acc[pl.ds(pl.multiple_of(corner * CELLS + t * 128, 128), 128), 0:128]
            for chunk in range(DEC_WIDE // 128):
                at = corner * DEC_WIDE + chunk * 128
                pick[to, at : at + 128] = ones_where(one == lanes + float(chunk * 128))

    @pl.loop(0, CELLS // TILE)
    def _(t):
        rows = pl.ds(pl.multiple_of(t * TILE, TILE), TILE)
        base = dot(cells[rows, :], w[15])
        for corner in range(3):
            at = corner * DEC_WIDE
            to = pl.ds(pl.multiple_of(corner * CELLS + t * TILE, TILE), TILE)
            acc[to, :] = base + dot(pick[rows, at : at + DEC_OWN], proj[ROUNDS, 0:DEC_OWN])

    for copy in got_near:
        copy.wait_recv()

    @pl.loop(0, CELLS // TILE)
    def _(t):
        rows = pl.ds(pl.multiple_of(t * TILE, TILE), TILE)
        totals = jnp.zeros((TILE, L), F32)
        for corner in range(3):
            at = corner * DEC_WIDE
            to = pl.ds(pl.multiple_of(corner * CELLS + t * TILE, TILE), TILE)
            before = acc[to, :] + dot(
                pick[rows, at + DEC_OWN : at + DEC_WIDE], near[ROUNDS].reshape(8 * BORDER, L)
            )
            totals = totals + norm(dot(hidden(before), w[OUT + 6]), gains[6:7, :])
        out[rows, :] = new_nodes(cells[rows, :], dot(cells[rows, :], w[16]), totals, 17, 7)

    for copy in sent:
        copy.wait_send()


def on_device(
    grid_latent, mesh_latent, edge_latent, g2m_src, g2m_dst, g2m_count, mesh_src, mesh_dst, m2g_src,
    weights_in, weights_out, gains,
):
    anywhere = pl.BlockSpec(memory_space=pl.ANY)
    vmem = pl.BlockSpec(memory_space=pltpu.VMEM)
    result = pl.pallas_call(
        kernel,
        out_shape=jax.ShapeDtypeStruct((CELLS, L), BF16),
        in_specs=[anywhere, vmem, anywhere] + [vmem] * 6 + [anywhere, anywhere, vmem],
        out_specs=vmem,
        scratch_shapes=[
            pltpu.VMEM((26, L, L), BF16),
            pltpu.VMEM((GRID_ROWS, L), BF16),
            pltpu.VMEM((2048, L), BF16),
            pltpu.VMEM((EDGE, L), BF16),
            pltpu.VMEM((3 * CELLS, L), F32),
            pltpu.VMEM((EDGE, WIDE), BF16),
            pltpu.VMEM((MESH, EDGE + G2M), BF16),
            pltpu.VMEM((ROUNDS, 2, 4, 4, 4, COARSE, L), BF16),
            pltpu.VMEM((ROUNDS + 1, 8, BORDER, L), BF16),
            pltpu.VMEM((ROUNDS + 1, 2 * MESH, L), BF16),
            pltpu.VMEM((G2M, L), BF16),
            pltpu.VMEM((MESH, L), BF16),
            pltpu.VMEM((MESH, L), F32),
            pltpu.VMEM((2, 16, L), BF16),
            pltpu.VMEM((128, 128), F32),
            pltpu.SemaphoreType.DMA((10,)),
            pltpu.SemaphoreType.DMA((120,)),
            pltpu.SemaphoreType.DMA((120,)),
        ],
        compiler_params=pltpu.CompilerParams(
            collective_id=0, has_side_effects=True, vmem_limit_bytes=62 * 1024 * 1024
        ),
        cost_estimate=pl.CostEstimate(flops=40_000_000_000, bytes_accessed=20_000_000, transcendentals=10_000_000),
    )(
        grid_latent.reshape(CELLS, L), mesh_latent.reshape(MESH, L), edge_latent.reshape(EDGE, L),
        g2m_src.reshape(1, G2M), g2m_dst.reshape(1, G2M), g2m_count,
        mesh_src.reshape(1, EDGE), mesh_dst.reshape(1, EDGE), m2g_src.reshape(-1, 128),
        weights_in, weights_out, gains,
    )
    return result.reshape(grid_latent.shape)


def solution(mesh):
    placed = (
        P("lat", "lon", None),
        P("lat", "lon", None, None),
        P("lat", "lon", None, None),
        P("lat", "lon", None),
        P("lat", "lon", None),
        P("lat", "lon"),
        P("lat", "lon", None),
        P("lat", "lon", None),
        P(None, "lat", "lon"),
        P(),
        P(),
        P(),
    )
    return jax.shard_map(
        on_device, mesh=mesh, in_specs=placed, out_specs=P("lat", "lon", None), check_vma=False
    )
```

time: 118 us -> 97.7 us (0.83)
  Pallas kernels: 109 us -> 94.6 us
  other arithmetic: 5.27 us -> 0 us
    pallas_call x1, Pallas kernels: 109 us -> 94.6 us  [on_device(): pl.pallas_call(kernel, out_shape=jax.ShapeDtypeStruct((CELLS, L), BF16),...]
    unnamed x4 -> x0, other arithmetic: 5.27 us -> none
where the time goes in v2:
time: 97.7 us; the launch traced here: 97.5 us
  Pallas kernels  94.6 us (97%)
  local copies, waits for them, and re-layouts  2.26 us (2%)
    pallas_call x1, Pallas kernels, on_device(): pl.pallas_call(kernel, out_shape=jax.ShapeDtypeStruct((CELLS, L), BF16),...  94.6 us
    unnamed x1, local copies, waits for them, and re-layouts  2.26 us

profile of v2, /device:TPU:0, one launch (start us, length us, event | category | flops | bytes accessed | tf_op | source)
XLA Modules:
  0.0 97.5 jit_solution(12050994621299351558)
XLA Ops:
  0.7 94.6 %shard_map.118 = bf16[1024,512]{1,0:T(8,128)(2,1)} custom-call(bf16[1024,512]{1,0:T(8,128)(2,1)} %bitcast.11, bf16[320,512]{1,0:T(8,128)(2,1)} %bitcast.12, bf16[2560,512]{1,0:T(8,128)(2,1)} %bitcast.10, s32[1,1536]{1,0:T(1,128)} %bitcast.16, s32[1,1536]{1,0:T(1,128)} %bitcast.17, s32[1,1]{1,0:T(1,128)S(6)} %copy.14.g2m_count, s32[1,2560]{1,0:T(1,128)} %bitcast.14, ...), custom_call_target="tpu_custom_call" | custom-call | flops 40000000000 | bytes 20000000 | tf_op jit(solution)/shard_map/pallas_call | solution.py:421
  95.2 2.3 %copy.15 = bf16[8,128,512]{2,1,0:T(8,128)(2,1)} copy(bf16[8,128,512]{2,1,0:T(8,128)(2,1)} %bitcast.9) | data formatting | bytes 2097152
